TPU v7x, 32 devices: a whole 2x2x4 slice. The times are simulated.
32 devices in a mesh: grp: 4 (over y, x), dp: 8 (over z, core).
Axes of the slice: x: 2, y: 2, z: 4, core: 2. Of those that a mesh axis runs over, the one named last changes fastest.
Arguments:
- queries: bfloat16 [4096, 2048], P(('grp', 'dp')), parts along dimension 0, may hold values from -96 to 96
- new_keys: bfloat16 [4096, 256], P(('grp', 'dp')), parts along dimension 0, may hold values from -5 to 5
- new_values: bfloat16 [4096, 256], P(('grp', 'dp')), parts along dimension 0, may hold values from -5 to 5
- cache_keys: bfloat16 [32768, 256], P(('grp', 'dp')), parts along dimension 0, may hold values from -5 to 5
- cache_values: bfloat16 [32768, 256], P(('grp', 'dp')), parts along dimension 0, may hold values from -5 to 5
- prefix_len: int32 [32], P(('grp', 'dp')), parts along dimension 0, may hold values from 1 to 1024, 4096 in all
- residual: bfloat16 [4096, 2048], P(('grp', 'dp')), parts along dimension 0, may hold values from -3 to 3
- out_weight: bfloat16 [2048, 2048], P('dp'), may hold values from -0.125 to 0.125
- norm_gain: float32 [2048], replicated, may hold values from 0.1 to 1.9
- expert_ids: int32 [4096, 4], P(('grp', 'dp')), parts along dimension 0, may hold values from 0 to 7, all different within a row; in each aligned block of 128 rows (0 to 127, 128 to 255, ...) at most 72 rows name the same one
- gate_scores: float32 [4096, 4], P(('grp', 'dp')), parts along dimension 0, may hold values from 0.05 to 1
- expert_gate_up: bfloat16 [8, 2048, 1536], P('dp'), may hold values from -0.125 to 0.125
- expert_down: bfloat16 [8, 768, 2048], P('dp'), may hold values from -0.21875 to 0.21875
Outputs:
- mixed: bfloat16 [4096, 2048], P(('grp', 'dp')), parts along dimension 0
There are 4 independent parts, one for each index of `grp`. A program takes and returns all parts, laid end to end along the dimension named above; an argument that names none is the same for every part. Nothing has to cross between parts.
Inputs may be any that keep to these rules, and one draw needn't show every extreme that they name: `expert_ids`: among the rows of one device each expert is named by at most 72 rows.
All inputs are finite; a program needn't handle non-finite values. No bound on the sum of `prefix_len` on one device may be relied on, other than what follows from the above.
Results may differ from a plain program's by a relative error of at most 0.0095.
Values may be sent and summed in bfloat16 or wider, within the bound.
A program may use at most 128 MiB of HBM per device.

v0:
```python
import jax
import jax.numpy as jnp
from jax import lax
from jax.sharding import PartitionSpec as P

D = 2048
HQ = 16
HK = 2
HD = 128
FF = 768
BLK = 256


NEGATIVE_FILL = -1e30


def block_step(state, query_heads, keys, vals, mask):
    top_old, sum_old, acc_old = state
    router_logits = jnp.einsum(
        "tgqd,kgd->tgqk", query_heads, keys, preferred_element_type=jnp.float32
    ) * HD ** (-0.5)
    wide_mask = mask[:, None, None, :]
    router_logits = jnp.where(wide_mask, router_logits, NEGATIVE_FILL)
    top_new = jnp.maximum(top_old, jnp.max(router_logits, axis=-1))
    expert_probabilities = jnp.where(wide_mask, jnp.exp(router_logits - top_new[..., None]), 0.0)
    shrink = jnp.exp(top_old - top_new)
    sum_new = sum_old * shrink + jnp.sum(expert_probabilities, axis=-1)
    acc_new = acc_old * shrink[..., None] + jnp.einsum(
        "tgqk,kgd->tgqd",
        expert_probabilities.astype(jnp.bfloat16),
        vals,
        preferred_element_type=jnp.float32,
    )
    return (top_new, sum_new, acc_new)


def prefix_range(state, query_heads, cache_k, cache_v, low, high):
    first = low // BLK
    last = (high + BLK - 1) // BLK

    def step(index, carry):
        start = index * BLK
        keys = lax.dynamic_slice_in_dim(cache_k, start, BLK, 0).reshape(BLK, HK, HD)
        vals = lax.dynamic_slice_in_dim(cache_v, start, BLK, 0).reshape(BLK, HK, HD)
        position = start + jnp.arange(BLK, dtype=jnp.int32)
        mask = ((position >= low) & (position < high))[None, :]
        return block_step(carry, query_heads, keys, vals, mask)

    return lax.fori_loop(first, last, step, state)


def empty_state(tok):
    group = HQ // HK
    return (
        jnp.full((tok, HK, group), NEGATIVE_FILL, jnp.float32),
        jnp.zeros((tok, HK, group), jnp.float32),
        jnp.zeros((tok, HK, group, HD), jnp.float32),
    )


def local(
    queries,
    new_keys,
    new_values,
    cache_keys,
    cache_values,
    prefix_len,
    residual,
    out_weight,
    norm_gain,
    expert_ids,
    gate_scores,
    expert_gate_up,
    expert_down,
):
    tok = queries.shape[0]
    group = HQ // HK
    query_heads = queries.reshape(tok, HK, group, HD)
    plen = prefix_len[0]
    state = prefix_range(
        empty_state(tok), query_heads, cache_keys, cache_values, jnp.int32(0), plen
    )
    row = jnp.arange(tok, dtype=jnp.int32)
    causal = row[None, :] <= row[:, None]
    state = block_step(
        state, query_heads, new_keys.reshape(tok, HK, HD), new_values.reshape(tok, HK, HD), causal
    )
    attended = (state[2] / state[1][..., None]).reshape(tok, HQ * HD).astype(jnp.bfloat16)
    projected = jnp.dot(
        attended,
        lax.all_gather(out_weight, "dp", axis=0, tiled=True),
        preferred_element_type=jnp.float32,
    )
    hidden_state = residual.astype(jnp.float32) + projected
    scale = lax.rsqrt(jnp.mean(hidden_state * hidden_state, axis=-1, keepdims=True) + 1e-06)
    normed = (hidden_state * scale * norm_gain).astype(jnp.bfloat16)
    choose = expert_ids.shape[1]
    count = expert_gate_up.shape[0] * lax.axis_size("dp")
    most = tok * choose // count * 9 // 8
    flat = expert_ids.reshape(-1)
    hits = (flat[:, None] == jnp.arange(count, dtype=jnp.int32)[None, :]).astype(jnp.int32)
    before = jnp.cumsum(hits, axis=0) - hits
    rank = jnp.sum(before * hits, axis=1)
    slot = flat * most + rank
    source_row = jnp.arange(flat.shape[0], dtype=jnp.int32) // choose
    source = jnp.zeros((count * most,), jnp.int32).at[slot].set(source_row)
    filled = jnp.zeros((count * most,), jnp.bool_).at[slot].set(True)
    outgoing = jnp.where(filled[:, None], normed[source], 0).reshape(count, most, D)
    weight_pair = expert_gate_up[0]
    weight_down = expert_down[0]
    pair = jnp.einsum(
        "smd,df->smf",
        lax.all_to_all(outgoing, "dp", split_axis=0, concat_axis=0, tiled=True),
        weight_pair,
        preferred_element_type=jnp.float32,
    )
    act = (jax.nn.silu(pair[..., :FF]) * pair[..., FF:]).astype(jnp.bfloat16)
    answered = jnp.einsum(
        "smf,fd->smd", act, weight_down, preferred_element_type=jnp.float32
    ).astype(jnp.bfloat16)
    returned_output = lax.all_to_all(answered, "dp", split_axis=0, concat_axis=0, tiled=True)
    picked = returned_output.reshape(count * most, D)[slot].reshape(tok, choose, D)
    route_weights = gate_scores / jnp.sum(gate_scores, axis=-1, keepdims=True)
    combined = jnp.sum(route_weights[:, :, None] * picked.astype(jnp.float32), axis=1)
    return (hidden_state + combined).astype(jnp.bfloat16)


def solution(mesh):
    in_specs = (
        P(("grp", "dp"), None),
        P(("grp", "dp"), None),
        P(("grp", "dp"), None),
        P(("grp", "dp"), None),
        P(("grp", "dp"), None),
        P(("grp", "dp")),
        P(("grp", "dp"), None),
        P("dp", None),
        P(),
        P(("grp", "dp"), None),
        P(("grp", "dp"), None),
        P("dp", None, None),
        P("dp", None, None),
    )
    out_specs = P(("grp", "dp"), None)
    return jax.shard_map(local, mesh=mesh, in_specs=in_specs, out_specs=out_specs, check_vma=False)
```

profile of v0, /device:TPU:0, one launch (start us, length us, event | category | flops | bytes accessed | tf_op | source)
XLA Modules:
  0.0 261.7 jit_solution(9197596820551266395)
XLA Ops:
  6.5 0.0 all-gather.2.cloned.1.call-start
  6.6 0.7 all-gather.2.cloned.1.call-update
  8.0 0.8 copy.32
  8.8 0.1 eq.29
  8.9 0.1 eq.25
  9.0 2.0 copy.22
  11.1 2.1 copy.24
  13.2 0.7 copy.45
  13.9 1.1 reduce-window.6
  15.1 0.2 slice_reduce_fusion
  15.3 0.0 copy-done.10
  15.3 0.1 copy.31
  15.4 0.1 mul.100
  15.6 0.1 fusion.38
  15.7 3.0 %scatter_custom_fusion.1 = s32[576]{0:T(1024)} fusion(s32[512]{0:T(512)S(1)} %bitcast.104, s32[512]{0:T(512)S(1)} %add_select_fusion, s32[]{:T(128)} %constant.79.clone.1), kind=kCustom, calls=%fused_computation.75 | custom fusion | bytes 2308 | tf_op jit(solution)/shard_map/scatter | solution.py:106
  18.7 2.4 scatter_custom_fusion
  21.1 0.7 broadcast_in_dim.95
  21.8 2.9 %fusion.49 = (f32[128,2,8]{0,2,1:T(8,128)}, f32[128,2,8,128]{0,3,2,1:T(8,128)}) fusion(bf16[128,2,8,128]{0,3,2,1:T(8,128)(2,1)} %bitcast.99, bf16[128,2,128,1]{2,1,0,3:T(2,128)(2,1)S(1)} %bitcast.102, pred[128,128]{0,1:T(8,128)(4,1)S(1)} %iota_compare_fusion), kind=kOutput, calls=%fused_computation.85 | convolution fusion | flops 67893248 | bytes 1662976 | tf_op jit(solution)/shard_map/tgqd,kgd->tgqk/dot_general | solution.py:19
  24.7 1.1 broadcast_in_dim.90
  25.8 9.2 %while.14 = (s32[]{:T(128)}, f32[128,2,8]{0,2,1:T(8,128)S(1)}, f32[128,2,8]{0,2,1:T(8,128)S(1)}, f32[128,2,8,128]{0,3,2,1:T(8,128)}, s32[]{:T(128)}, /*index=5*/...) while((s32[]{:T(128)}, f32[128,2,8]{0,2,1:T(8,128)S(1)}, ...), condition=%wide.region_3.4_spmd, body=%wide.region_0.3_spmd.sunk | while | flops 275780608 | bytes 18744532 | solution.py:49
  25.9 1.0 constant_dynamic-slice_fusion.3
  26.8 0.1 copy.54
  27.0 0.7 compare_and_fusion.2
  27.6 1.6 bitcast_reduce_fusion.2
  29.2 1.4 copy-done.1
  30.6 0.6 fusion.68
  31.3 0.1 copy.55
  31.4 3.6 %fusion.69 = f32[128,2,8,128]{0,3,2,1:T(8,128)} fusion(bf16[256,2,128,1]{0,2,3,1:T(8,128)(2,1)S(1)} %bitcast.100, f32[2,256,128,8]{2,1,3,0:T(8,128)} %copy-done.1, f32[128,2,8,128]{0,3,2,1:T(8,128)} %get-tuple-element.190, f32[128,2,8]{0,2,1:T(8,128)S(1)} %max.8, pred[256]{0:T(512)(128)(4,1)S(1)} %compare_and_fusion.2, ...), kind=kOutput, calls=%fused_computation.12.clone.1 | convolution fusion | flops 137363456 | bytes 4342016 | tf_op jit(solution)/shard_map/while/body/tgqk,kgd->tgqd/dot_general | solution.py:28
  35.0 0.7 max.6
  35.7 0.7 compare_select_fusion.1
  36.4 1.5 fusion.30
  37.9 2.7 %fusion.27 = bf16[128,2,8,128]{0,3,2,1:T(8,128)(2,1)} fusion(bf16[128,2,128,1]{0,2,3,1:T(8,128)(2,1)} %bitcast.103, f32[128,2,8,128]{0,3,2,1:T(8,128)} %get-tuple-element.55, f32[128,2,8,128]{0,3,2,1:T(8,128)} %get-tuple-element.103, f32[128,2,8]{0,2,1:T(8,128)S(1)} %get-tuple-element.96, f32[128,2,8]{0,2,1:T(8,128)S(1)} %max.6, ...), kind=kOutput, calls=%fused_computation.43 | convolution fusion | flops 68943872 | bytes 2727936 | tf_op jit(solution)/shard_map/tgqk,kgd->tgqd/dot_general | solution.py:28
  40.6 53.1 %all-gather.2.cloned.1.call-done = bf16[2048,2048]{1,0:T(8,128)(2,1)} async-done(((bf16[256,2048]{1,0:T(8,128)(2,1)}), bf16[2048,2048]{1,0:T(8,128)(2,1)}) %all-gather.2.cloned.1.call-update) | async-done | bytes 8388624 | tf_op jit(solution)/shard_map/all_gather | solution.py:91
  93.8 4.9 %multiply_reduce_fusion.1 = (f32[128]{0:T(128)S(1)}, f32[128,2048]{1,0:T(8,128)S(1)}) fusion(bf16[128,2048]{0,1:T(8,128)(2,1)} %bitcast.101, bf16[2048,2048]{1,0:T(8,128)(2,1)} %all-gather.2.cloned.1.call-done, bf16[128,2048]{1,0:T(8,128)(2,1)} %param.21), kind=kOutput, calls=%fused_computation.46 | convolution fusion | flops 1074790272 | bytes 10486272 | tf_op jit(solution)/shard_map/dot_general | solution.py:89
  98.7 1.0 copy-done.2
  99.7 0.9 multiply_convert_fusion
  100.7 8.0 %gather_fusion = bf16[576,2048]{1,0:T(8,128)(2,1)} fusion(bf16[128,2048]{1,0:T(8,128)(2,1)} %multiply_convert_fusion, s32[1024]{0:T(1024)S(1)} %pad_clamp_fusion.1), kind=kCustom, calls=%fused_computation | custom fusion | bytes 4720896 | tf_op jit(solution)/shard_map/gather | solution.py:108
  108.6 1.9 broadcast_select_fusion
  110.5 57.1 %all_to_all.10 = bf16[8,72,2048]{2,1,0:T(8,128)(2,1)S(1)} all-to-all(bf16[8,72,2048]{2,1,0:T(8,128)(2,1)S(1)} %broadcast_select_fusion), channel_id=1, replica_groups=mesh['grp'=4,'dp'=8] {'dp'}, dimensions={0} | all-to-all | bytes 4718592 | tf_op jit(solution)/shard_map/all_to_all | solution.py:113
  167.7 6.1 %fusion.15 = f32[8,72,1536]{2,1,0:T(8,128)S(1)} fusion(bf16[8,72,2048]{2,1,0:T(8,128)(2,1)S(1)} %all_to_all.10, bf16[1,2048,1536]{2,1,0:T(8,128)(2,1)} %param.26), kind=kOutput, calls=%fused_computation.27 | convolution fusion | flops 3623878656 | bytes 12189696 | tf_op jit(solution)/shard_map/smd,df->smf/dot_general | solution.py:111
  173.7 3.5 %fusion.19 = bf16[8,72,2048]{2,1,0:T(8,128)(2,1)} fusion(bf16[1,768,2048]{2,1,0:T(8,128)(2,1)S(1)} %copy-done, f32[8,72,1536]{2,1,0:T(8,128)S(1)} %fusion.15), kind=kOutput, calls=%fused_computation.32 | convolution fusion | flops 1815773184 | bytes 9043968 | tf_op jit(solution)/shard_map/smf,fd->smd/dot_general | solution.py:118
  177.2 4.5 %all-to-all-start.1 = ((bf16[8,72,2048]{2,1,0:T(8,128)(2,1)}), bf16[8,72,2048]{2,1,0:T(8,128)(2,1)}, u32[]{:S(2)}, u32[]{:S(2)}) async-start(bf16[8,72,2048]{2,1,0:T(8,128)(2,1)} %fusion.19), calls=%async_computation.1 | async-start | bytes 4718592 | tf_op jit(solution)/shard_map/all_to_all | solution.py:121
  181.8 0.1 copy.30
  181.9 54.5 %all-to-all-done.1 = bf16[8,72,2048]{2,1,0:T(8,128)(2,1)} async-done(((bf16[8,72,2048]{2,1,0:T(8,128)(2,1)}), bf16[8,72,2048]{2,1,0:T(8,128)(2,1)}, u32[]{:S(2)}, u32[]{:S(2)}) %all-to-all-start.1) | async-done | bytes 2359328 | tf_op jit(solution)/shard_map/all_to_all | solution.py:121
  236.4 7.2 %gather_fusion.1 = bf16[512,2048]{1,0:T(8,128)(2,1)} fusion(bf16[576,2048]{1,0:T(8,128)(2,1)} %bitcast.25, s32[1024]{0:T(1024)S(1)} %pad_clamp_fusion), kind=kCustom, calls=%fused_computation.1 | custom fusion | bytes 4196352 | tf_op jit(solution)/shard_map/gather | solution.py:122
  243.7 4.8 %reshape.116 = f32[128,4,2048]{2,1,0:T(4,128)} reshape(bf16[512,2048]{1,0:T(8,128)(2,1)} %gather_fusion.1) | data formatting | bytes 6291456 | tf_op jit(solution)/shard_map/convert_element_type | solution.py:124
  248.4 5.5 %multiply_reduce_fusion = f32[128,2048]{1,0:T(8,128)S(1)} fusion(f32[128,4,2048]{2,1,0:T(4,128)} %reshape.116, f32[128,4]{1,0:T(8,128)S(1)} %copy.30), kind=kLoop, calls=%fused_computation.29 | loop fusion | flops 1835008 | bytes 5244928 | tf_op jit(solution)/shard_map/reduce_sum | solution.py:124
  253.9 0.9 add_convert_fusion
  (43 shorter events, 0.2 us)
Async XLA Ops:
  6.5 167.2 %copy-start = (bf16[1,768,2048]{2,1,0:T(8,128)(2,1)S(1)}, bf16[1,768,2048]{2,1,0:T(8,128)(2,1)}, u32[]{:S(2)}) copy-start(bf16[1,768,2048]{2,1,0:T(8,128)(2,1)} %param.27) | copy-start | bytes 9437188
  6.5 8.8 %copy-start.10 = (s32[128,4]{0,1:T(4,128)S(1)}, s32[128,4]{0,1:T(4,128)}, u32[]{:S(2)}) copy-start(s32[128,4]{0,1:T(4,128)} %param.24) | copy-start | bytes 6148
  6.5 6.6 %copy-start.5 = (bf16[128,256]{1,0:T(8,128)(2,1)S(1)}, bf16[128,256]{1,0:T(8,128)(2,1)}, u32[]{:S(2)}) copy-start(bf16[128,256]{1,0:T(8,128)(2,1)} %param.16) | copy-start | bytes 196612
  6.5 6.6 %copy-start.6 = (bf16[128,256]{1,0:T(8,128)(2,1)S(1)}, bf16[128,256]{1,0:T(8,128)(2,1)}, u32[]{:S(2)}) copy-start(bf16[128,256]{1,0:T(8,128)(2,1)} %param.17) | copy-start | bytes 196612
  6.5 87.2 %all-gather.2.cloned.1.call-start = ((), (), s32[]{:S(2)}) async-start(), calls=%async_computation.2 | async-start | bytes 9437184 | tf_op jit(solution)/shard_map/all_gather | solution.py:91
  15.7 10.2 %copy-start.8 = (s32[512,1]{0,1:T(1,128)}, s32[512,1]{0,1:T(1,128)S(1)}, u32[]{:S(2)}) copy-start(s32[512,1]{0,1:T(1,128)S(1)} %compare_select_fusion) | copy-start | bytes 6148
  21.8 4.0 %copy-start.4 = (pred[128,128]{0,1:T(8,128)(4,1)}, pred[128,128]{0,1:T(8,128)(4,1)S(1)}, u32[]{:S(2)}) copy-start(pred[128,128]{0,1:T(8,128)(4,1)S(1)} %iota_compare_fusion) | copy-start | bytes 49156
  29.2 1.4 copy-start.1
  93.8 6.0 %copy-start.7 = (f32[2048]{0:T(1024)S(1)}, f32[2048]{0:T(1024)}, u32[]{:S(2)}) copy-start(f32[2048]{0:T(1024)} %param.23) | copy-start | bytes 24580
  98.7 1.0 copy-start.2
  100.7 8.0 %copy-start.12 = (pred[8,72]{1,0:T(8,128)(4,1)S(1)}, pred[8,72]{1,0:T(8,128)(4,1)}, u32[]{:S(2)}) copy-start(pred[8,72]{1,0:T(8,128)(4,1)} %broadcast_in_dim.95) | copy-start | bytes 1732
  177.2 4.5 %copy-start.11 = (f32[128,4]{0,1:T(4,128)S(1)}, f32[128,4]{0,1:T(4,128)}, u32[]{:S(2)}) copy-start(f32[128,4]{0,1:T(4,128)} %param.25) | copy-start | bytes 6148
  177.2 4.7 %copy-start.9 = (s32[512,1]{0,1:T(1,128)S(1)}, s32[512,1]{0,1:T(1,128)}, u32[]{:S(2)}) copy-start(s32[512,1]{0,1:T(1,128)} %copy-done.8) | copy-start | bytes 6148
  177.2 59.2 %all-to-all-start.1 = ((bf16[8,72,2048]{2,1,0:T(8,128)(2,1)}), bf16[8,72,2048]{2,1,0:T(8,128)(2,1)}, u32[]{:S(2)}, u32[]{:S(2)}) async-start(bf16[8,72,2048]{2,1,0:T(8,128)(2,1)} %fusion.19), calls=%async_computation.1 | async-start | bytes 4718592 | tf_op jit(solution)/shard_map/all_to_all | solution.py:121
  248.4 5.5 %copy-start.3 = (f32[128,2048]{1,0:T(8,128)S(1)}, f32[128,2048]{1,0:T(8,128)}, u32[]{:S(2)}) copy-start(f32[128,2048]{1,0:T(8,128)} %copy-done.2) | copy-start | bytes 3145732
Sparse Core Ops, SparseCore 0:
  9.0 84.7 all-gather.1
where the time goes:
time: 263 us; the launch traced here: 262 us
  waiting for transfers between devices  108 us (41%)
  blocking collectives  57.1 us (22%)
  local copies, waits for them, and re-layouts  37.2 us (14%)
  matrix products  25.4 us (10%)
  other arithmetic  14.7 us (6%)
  between operations  14.3 us (5%)
  starting transfers between devices  4.53 us (2%)
    all_to_all x1, blocking collectives, local(): lax.all_to_all(outgoing, 'dp', split_axis=0, concat_axis=0, tiled=True)  57.1 us
    all_to_all x1, waiting for transfers between devices, local(): lax.all_to_all(answered, 'dp', split_axis=0, concat_axis=0, tiled=True)  54.5 us
    all_gather x1, waiting for transfers between devices, local(): lax.all_gather(out_weight, 'dp', axis=0, tiled=True)  53.1 us
    gather x1, local copies, waits for them, and re-layouts, local(): normed[source]  7.96 us
    gather x1, local copies, waits for them, and re-layouts, local(): returned_output.reshape(count * most, D)[slot].reshape(tok, choose, D)  7.24 us
    dot_general x2, matrix products, block_step(): jnp.einsum('tgqk,kgd->tgqd', expert_probabilities.astype(jnp.bfloat16), v...  6.39 us
    dot_general x1, matrix products, local(): jnp.einsum('smd,df->smf', lax.all_to_all(outgoing, 'dp', split_axis=0, co...  6.05 us
    reduce_sum x1, other arithmetic, local(): jnp.sum(route_weights[:, :, None] * picked.astype(jnp.float32), axis=1)  5.5 us
  transfers between devices with their start and end apart: 2, of which 2 were waited for; matrix products, arithmetic and copies ran while one was open for 12% of the time, Pallas kernels for 0%

commit v1 on v0

--- a/solution.py
+++ b/solution.py
@@ -1,6 +1,10 @@
+import functools
+
 import jax
 import jax.numpy as jnp
 from jax import lax
+from jax.experimental import pallas as pl
+from jax.experimental.pallas import tpu as pltpu
 from jax.sharding import PartitionSpec as P
 
 D = 2048
@@ -56,6 +60,236 @@
         jnp.zeros((tok, HK, group), jnp.float32),
         jnp.zeros((tok, HK, group, HD), jnp.float32),
     )
+
+
+SPLIT = 2
+VMEM_BYTES = 58 * 1024 * 1024
+
+
+def block_at(p, z, nz):
+    both = jnp.minimum(z, nz - 1 - z)
+    half = (p + 1) // 2
+    near = jnp.where(p % 2 == 1, z - half, z + half)
+    far = jnp.where(z > nz - 1 - z, z - (p - both), z + (p - both))
+    return jnp.where(p <= 2 * both, near, far)
+
+
+def experts_kernel(
+    nz, split, x_ref, hidden_ref, share_ref, gu_hbm, down_hbm, out_ref,
+    gu, down, xs, ys, sib_sum, line_sum, total, act, acc,
+    load_sem, x_send, x_recv, xsib_send, xsib_recv, ysib_send, ysib_recv, line_send, line_recv,
+):
+    me = lax.axis_index("dp")
+    z, c = me // 2, me % 2
+    other = 1 - c
+    sibling = 2 * z + other
+    right, left = me + 2, me - 2
+    rows = xs.shape[3]
+    width = xs.shape[4]
+    hidden_units = down.shape[0]
+    has_left, has_right = z > 0, z < nz - 1
+
+    load_gu = pltpu.make_async_copy(gu_hbm, gu, load_sem.at[0])
+    load_down = pltpu.make_async_copy(down_hbm, down, load_sem.at[1])
+    load_gu.start()
+    load_down.start()
+    for s in range(split):
+        xs[z, s, c] = x_ref[s]
+
+    barrier = pltpu.get_barrier_semaphore()
+
+    def greet(device):
+        pl.semaphore_signal(
+            barrier, inc=1, device_id={"dp": device}, device_id_type=pl.DeviceIdType.MESH
+        )
+
+    greet(sibling)
+    pl.when(has_left)(lambda: greet(left))
+    pl.when(has_right)(lambda: greet(right))
+    pl.semaphore_wait(barrier, 1 + jnp.where(has_left, 1, 0) + jnp.where(has_right, 1, 0))
+
+    def remote(src, dst, send, recv, device):
+        return pltpu.make_async_remote_copy(
+            src_ref=src, dst_ref=dst, send_sem=send, recv_sem=recv,
+            device_id={"dp": device}, device_id_type=pl.DeviceIdType.MESH,
+        )
+
+    def x_line(b, s, way, device):
+        return remote(xs.at[b, s, c], xs.at[b, s, c], x_send.at[way, b, s], x_recv.at[b, s], device)
+
+    def x_sib(b, s, core):
+        return remote(
+            xs.at[b, s, core], xs.at[b, s, core], xsib_send.at[b, s], xsib_recv.at[b, s], sibling
+        )
+
+    def y_sib(b, s):
+        return remote(
+            ys.at[b, s, other], sib_sum.at[b, s], ysib_send.at[b, s], ysib_recv.at[b, s], sibling
+        )
+
+    def sum_line(b, s, way, device):
+        return remote(
+            total.at[b, s], line_sum.at[way, b, s], line_send.at[b, s], line_recv.at[way, b, s], device
+        )
+
+    def send_own(s, carry):
+        pl.when(has_right)(lambda: x_line(z, s, 0, right).start())
+        pl.when(has_left)(lambda: x_line(z, s, 1, left).start())
+        x_sib(z, s, c).start()
+        return carry
+
+    lax.fori_loop(0, split, send_own, 0)
+    load_gu.wait()
+    load_down.wait()
+
+    def send_sum(b, s):
+        pl.when(b > z)(lambda: sum_line(b, s, 0, right).start())
+        pl.when(b < z)(lambda: sum_line(b, s, 1, left).start())
+
+    def is_end(b):
+        return ((b > z) & (z == 0)) | ((b < z) & (z == nz - 1))
+
+    def compute(i, carry):
+        p, s = i // split, i % split
+        b = block_at(p, z, nz)
+
+        @pl.when(p > 0)
+        def _():
+            x_line(b, s, 0, sibling).wait_recv()
+            pl.when((b < z) & has_right)(lambda: x_line(b, s, 0, right).start())
+            pl.when((b > z) & has_left)(lambda: x_line(b, s, 1, left).start())
+            x_sib(b, s, c).start()
+
+        x_sib(b, s, other).wait_recv()
+        x = xs[b, s].reshape(2 * rows, width)
+        tile = 256
+        for f in range(0, hidden_units, tile):
+            gate = jnp.dot(x, gu[:, f : f + tile], preferred_element_type=jnp.float32)
+            up = jnp.dot(
+                x, gu[:, hidden_units + f : hidden_units + f + tile],
+                preferred_element_type=jnp.float32,
+            )
+            act[:, f : f + tile] = (gate / (1.0 + jnp.exp(-gate)) * up).astype(jnp.bfloat16)
+        share = share_ref[b, s]
+        for d in range(0, width, 512):
+            y = jnp.dot(act[...], down[:, d : d + 512], preferred_element_type=jnp.float32)
+            ys[b, s, :, :, d : d + 512] = (
+                (y * share).astype(jnp.bfloat16).reshape(2, rows, 512)
+            )
+        y_sib(b, s).start()
+
+        @pl.when(is_end(b))
+        def _():
+            y_sib(b, s).wait_recv()
+            total[b, s] = (
+                ys[b, s, c].astype(jnp.float32) + sib_sum[b, s].astype(jnp.float32)
+            ).astype(jnp.bfloat16)
+            send_sum(b, s)
+
+        return carry
+
+    lax.fori_loop(0, nz * split, compute, 0)
+
+    def add_and_pass(b, s, way):
+        y_sib(b, s).wait_recv()
+        sum_line(b, s, way, sibling).wait_recv()
+        total[b, s] = (
+            ys[b, s, c].astype(jnp.float32)
+            + sib_sum[b, s].astype(jnp.float32)
+            + line_sum[way, b, s].astype(jnp.float32)
+        ).astype(jnp.bfloat16)
+        send_sum(b, s)
+
+    def pass_on(i, carry):
+        hop, s = i // split, i % split
+        from_left, from_right = hop - z, 2 * (nz - 1) - z - hop
+        pl.when(has_left & (from_left > z) & (from_left < nz))(lambda: add_and_pass(from_left, s, 0))
+        pl.when(has_right & (from_right < z) & (from_right >= 0))(
+            lambda: add_and_pass(from_right, s, 1)
+        )
+        return carry
+
+    lax.fori_loop(split, (2 * nz - 1) * split, pass_on, 0)
+
+    def finish(s, carry):
+        y_sib(z, s).wait_recv()
+        acc[...] = (
+            hidden_ref[s] + ys[z, s, c].astype(jnp.float32) + sib_sum[z, s].astype(jnp.float32)
+        )
+
+        @pl.when(has_left)
+        def _():
+            sum_line(z, s, 0, sibling).wait_recv()
+            acc[...] += line_sum[0, z, s].astype(jnp.float32)
+
+        @pl.when(has_right)
+        def _():
+            sum_line(z, s, 1, sibling).wait_recv()
+            acc[...] += line_sum[1, z, s].astype(jnp.float32)
+
+        out_ref[s] = acc[...].astype(out_ref.dtype)
+        return carry
+
+    lax.fori_loop(0, split, finish, 0)
+
+    def drain(i, carry):
+        b, s = i // split, i % split
+        pl.when((b <= z) & has_right)(lambda: x_line(b, s, 0, right).wait_send())
+        pl.when((b >= z) & has_left)(lambda: x_line(b, s, 1, left).wait_send())
+        x_sib(b, s, c).wait_send()
+        y_sib(b, s).wait_send()
+        pl.when(b != z)(lambda: sum_line(b, s, 0, sibling).wait_send())
+        return carry
+
+    lax.fori_loop(0, nz * split, drain, 0)
+
+
+def experts(normed, hidden_state, share, gate_up, down):
+    tok, width = normed.shape
+    n_dp = lax.axis_size("dp")
+    nz, split = n_dp // 2, SPLIT
+    rows = tok // split
+    units = down.shape[0]
+    share = share.reshape(nz, 2, split, rows).transpose(0, 2, 1, 3).reshape(nz, split, 2 * rows, 1)
+    vmem = pl.BlockSpec(memory_space=pltpu.VMEM)
+    hbm = pl.BlockSpec(memory_space=pl.ANY)
+    half = jnp.bfloat16
+    dma = pltpu.SemaphoreType.DMA
+    out = pl.pallas_call(
+        functools.partial(experts_kernel, nz, split),
+        out_shape=jax.ShapeDtypeStruct((split, rows, width), half),
+        in_specs=[vmem, vmem, vmem, hbm, hbm],
+        out_specs=vmem,
+        scratch_shapes=[
+            pltpu.VMEM(gate_up.shape, half),
+            pltpu.VMEM(down.shape, half),
+            pltpu.VMEM((nz, split, 2, rows, width), half),
+            pltpu.VMEM((nz, split, 2, rows, width), half),
+            pltpu.VMEM((nz, split, rows, width), half),
+            pltpu.VMEM((2, nz, split, rows, width), half),
+            pltpu.VMEM((nz, split, rows, width), half),
+            pltpu.VMEM((2 * rows, units), half),
+            pltpu.VMEM((rows, width), jnp.float32),
+            dma((2,)),
+            dma((2, nz, split)),
+            dma((nz, split)),
+            dma((nz, split)),
+            dma((nz, split)),
+            dma((nz, split)),
+            dma((nz, split)),
+            dma((nz, split)),
+            dma((2, nz, split)),
+        ],
+        compiler_params=pltpu.CompilerParams(
+            collective_id=1, has_side_effects=True, vmem_limit_bytes=VMEM_BYTES
+        ),
+        name="experts",
+    )(
+        normed.reshape(split, rows, width),
+        hidden_state.reshape(split, rows, width),
+        share, gate_up, down,
+    )
+    return out.reshape(tok, width)
 
 
 def local(
@@ -94,35 +328,14 @@
     hidden_state = residual.astype(jnp.float32) + projected
     scale = lax.rsqrt(jnp.mean(hidden_state * hidden_state, axis=-1, keepdims=True) + 1e-06)
     normed = (hidden_state * scale * norm_gain).astype(jnp.bfloat16)
-    choose = expert_ids.shape[1]
     count = expert_gate_up.shape[0] * lax.axis_size("dp")
-    most = tok * choose // count * 9 // 8
-    flat = expert_ids.reshape(-1)
-    hits = (flat[:, None] == jnp.arange(count, dtype=jnp.int32)[None, :]).astype(jnp.int32)
-    before = jnp.cumsum(hits, axis=0) - hits
-    rank = jnp.sum(before * hits, axis=1)
-    slot = flat * most + rank
-    source_row = jnp.arange(flat.shape[0], dtype=jnp.int32) // choose
-    source = jnp.zeros((count * most,), jnp.int32).at[slot].set(source_row)
-    filled = jnp.zeros((count * most,), jnp.bool_).at[slot].set(True)
-    outgoing = jnp.where(filled[:, None], normed[source], 0).reshape(count, most, D)
-    weight_pair = expert_gate_up[0]
-    weight_down = expert_down[0]
-    pair = jnp.einsum(
-        "smd,df->smf",
-        lax.all_to_all(outgoing, "dp", split_axis=0, concat_axis=0, tiled=True),
-        weight_pair,
-        preferred_element_type=jnp.float32,
-    )
-    act = (jax.nn.silu(pair[..., :FF]) * pair[..., FF:]).astype(jnp.bfloat16)
-    answered = jnp.einsum(
-        "smf,fd->smd", act, weight_down, preferred_element_type=jnp.float32
-    ).astype(jnp.bfloat16)
-    returned_output = lax.all_to_all(answered, "dp", split_axis=0, concat_axis=0, tiled=True)
-    picked = returned_output.reshape(count * most, D)[slot].reshape(tok, choose, D)
     route_weights = gate_scores / jnp.sum(gate_scores, axis=-1, keepdims=True)
-    combined = jnp.sum(route_weights[:, :, None] * picked.astype(jnp.float32), axis=1)
-    return (hidden_state + combined).astype(jnp.bfloat16)
+    chosen = expert_ids[:, :, None] == jnp.arange(count, dtype=jnp.int32)
+    share = jnp.sum(jnp.where(chosen, route_weights[:, :, None], 0.0), axis=1)
+    shares = lax.all_gather(share, "dp", axis=0, tiled=True)
+    mine = jnp.arange(count, dtype=jnp.int32) == lax.axis_index("dp")
+    share = jnp.sum(jnp.where(mine, shares, 0.0), axis=1)
+    return experts(normed, hidden_state, share, expert_gate_up[0], expert_down[0])
 
 
 def solution(mesh):

time: 263 us -> 178 us (0.68)
  Pallas kernels: 0 us -> 69.1 us
  waiting for transfers between devices: 108 us -> 55.5 us
  blocking collectives: 57.1 us -> 15.8 us
  local copies, waits for them, and re-layouts: 37.2 us -> 7.36 us
  matrix products: 25.4 us -> 11.6 us
  other arithmetic: 14.7 us -> 4 us
  starting transfers between devices: 4.53 us -> 0.03 us
    pallas_call x0 -> x1, Pallas kernels: none -> 69.1 us  [experts(): pl.pallas_call(functools.partial(experts_kernel, nz, split), out_shape=ja...]
    all_to_all x1 -> x0, blocking collectives: 57.1 us -> none  [local(): lax.all_to_all(outgoing, 'dp', split_axis=0, concat_axis=0, tiled=True)]
    all_to_all x1 -> x0, waiting for transfers between devices: 54.5 us -> none  [local(): lax.all_to_all(answered, 'dp', split_axis=0, concat_axis=0, tiled=True)]
    all_gather x0 -> x1, blocking collectives: none -> 15.8 us  [local(): shares = lax.all_gather(share, 'dp', axis=0, tiled=True)]
    gather x2 -> x0, local copies, waits for them, and re-layouts: 15.2 us -> none  [the longest x1 7.96 us: local(): normed[source]]
    dot_general x2 -> x0, matrix products: 9.53 us -> none  [the longest x1 6.05 us: local(): jnp.einsum('smd,df->smf', lax.all_to_all(outgoing, 'dp', split_axis=0, co...]
    reduce_sum x2, other arithmetic: 5.59 us -> 0.09 us  [the longest x1 0.08 us: local(): share = jnp.sum(jnp.where(mine, shares, 0.0), axis=1)]
    scatter x2 -> x0, local copies, waits for them, and re-layouts: 5.45 us -> none  [the longest x1 3.01 us: local(): source = jnp.zeros((count * most,), jnp.int32).at[slot].set(source_row)]
  transfers between devices with their start and end apart: 2 -> 1, of which waited for: 2 -> 1; matrix products, arithmetic and copies ran while one was open for 12% -> 9% of each run, Pallas kernels for 0% -> 0%
where the time goes in v1:
time: 178 us
  Pallas kernels  69.1 us (39%)
  waiting for transfers between devices  55.5 us (31%)
  blocking collectives  15.8 us (9%)
  between operations  14.2 us (8%)
  matrix products  11.6 us (7%)
  local copies, waits for them, and re-layouts  7.36 us (4%)
  other arithmetic  4 us (2%)
    pallas_call x1, Pallas kernels, experts(): pl.pallas_call(functools.partial(experts_kernel, nz, split), out_shape=ja...  69.1 us
    all_gather x1, waiting for transfers between devices, local(): lax.all_gather(out_weight, 'dp', axis=0, tiled=True)  54.8 us
    all_gather x1, blocking collectives, local(): shares = lax.all_gather(share, 'dp', axis=0, tiled=True)  15.8 us
    dot_general x2, matrix products, block_step(): jnp.einsum('tgqk,kgd->tgqd', expert_probabilities.astype(jnp.bfloat16), v...  4.89 us
    dot_general x1, matrix products, local(): jnp.dot(attended, lax.all_gather(out_weight, 'dp', axis=0, tiled=True), p...  4.75 us
  transfers between devices with their start and end apart: 1, of which 1 were waited for; matrix products, arithmetic and copies ran while one was open for 9% of the time, Pallas kernels for 0%

profile of v1, /device:TPU:0, one launch (start us, length us, event | category | flops | bytes accessed | tf_op | source)
XLA Modules:
  0.0 177.5 jit_solution(15163560892491132200)
XLA Ops:
  6.5 0.0 copy-start.2
  6.5 0.0 copy-start.3
  6.5 0.0 copy-start.5
  6.5 0.0 copy-start.6
  6.5 0.0 all-gather.2.cloned.1.call-start
  6.6 0.7 all-gather.2.cloned.1.call-update
  7.9 1.3 copy.37
  9.3 0.3 copy.39
  9.5 0.0 copy-done.2
  9.6 0.0 copy-done.3
  9.6 0.1 copy.58
  9.7 0.0 copy-done.5
  9.8 0.0 copy-done.6
  9.8 15.8 %all_gather.7 = f32[1024,8]{0,1:T(8,128)S(1)} all-gather(f32[128,8]{0,1:T(8,128)S(1)} %select_reduce_fusion.1), channel_id=1, replica_groups=mesh['grp'=4,'dp'=8] {'dp'}, dimensions={0}, use_global_device_ids=true | all-gather | bytes 36864 | tf_op jit(solution)/shard_map/all_gather | solution.py:335
  25.5 0.1 select_reduce_fusion
  25.6 0.1 reshape.72
  25.7 1.3 reshape.79.share_ref
  27.1 1.4 fusion.28
  28.4 1.1 broadcast_in_dim.84
  29.5 6.0 %while.14 = (s32[]{:T(128)}, f32[128,2,8]{0,2,1:T(8,128)S(1)}, f32[128,2,8]{0,2,1:T(8,128)S(1)}, f32[128,2,8,128]{0,3,2,1:T(8,128)}, s32[]{:T(128)}, /*index=5*/...) while((s32[]{:T(128)}, f32[128,2,8]{0,2,1:T(8,128)S(1)}, ...), condition=%wide.region_3.4_spmd, body=%wide.region_0.3_spmd.sunk | while | flops 275780608 | bytes 10355895 | solution.py:53
  29.5 1.0 constant_dynamic-slice_fusion.3
  30.5 0.1 copy.67
  30.6 0.7 compare_and_fusion.2
  31.3 0.6 bitcast_reduce_fusion.2
  31.8 0.6 fusion.46
  32.5 0.1 copy.68
  32.6 2.9 %fusion.47 = f32[128,2,8,128]{0,3,2,1:T(8,128)} fusion(bf16[256,2,128,1]{0,2,3,1:T(8,128)(2,1)S(1)} %bitcast.84, f32[2,256,128,8]{2,1,3,0:T(8,128)S(1)} %get-tuple-element.179, f32[128,2,8,128]{0,3,2,1:T(8,128)} %get-tuple-element.199, f32[128,2,8]{0,2,1:T(8,128)S(1)} %max.8, pred[256]{0:T(512)(128)(4,1)S(1)} %compare_and_fusion.2, ...), kind=kOutput, calls=%fused_computation.8.clone.1 | convolution fusion | flops 137363456 | bytes 4342016 | tf_op jit(solution)/shard_map/while/body/tgqk,kgd->tgqd/dot_general | solution.py:32
  35.6 1.4 fusion.20
  37.0 0.0 copy-start.1
  37.0 1.9 %fusion.19 = bf16[128,2,8,128]{0,3,2,1:T(8,128)(2,1)S(1)} fusion(bf16[128,2,128,1]{0,2,3,1:T(8,128)(2,1)S(1)} %bitcast.90, f32[128,2,8,128]{0,3,2,1:T(8,128)} %get-tuple-element.55, f32[128,2,8,128]{0,3,2,1:T(8,128)} %get-tuple-element.112, f32[128,2,8]{0,2,1:T(8,128)S(1)} %get-tuple-element.105, f32[128,2,8]{0,2,1:T(8,128)S(1)} %max.6, ...), kind=kOutput, calls=%fused_computation.30 | convolution fusion | flops 68943872 | bytes 2727936 | tf_op jit(solution)/shard_map/tgqk,kgd->tgqd/dot_general | solution.py:32
  39.0 54.8 %all-gather.2.cloned.1.call-done = bf16[2048,2048]{1,0:T(8,128)(2,1)} async-done(((bf16[256,2048]{1,0:T(8,128)(2,1)}), bf16[2048,2048]{1,0:T(8,128)(2,1)}) %all-gather.2.cloned.1.call-update) | async-done | bytes 8388624 | tf_op jit(solution)/shard_map/all_gather | solution.py:325
  93.8 0.0 copy-done.1
  93.8 0.0 copy-start.4
  93.8 4.8 %multiply_reduce_fusion = (f32[128]{0:T(128)S(1)}, f32[128,2048]{1,0:T(8,128)S(1)}) fusion(bf16[128,2048]{0,1:T(8,128)(2,1)S(1)} %bitcast.88, bf16[2048,2048]{1,0:T(8,128)(2,1)} %all-gather.2.cloned.1.call-done, bf16[128,2048]{1,0:T(8,128)(2,1)S(1)} %copy-done.1), kind=kOutput, calls=%fused_computation.32 | convolution fusion | flops 1074790272 | bytes 10486272 | tf_op jit(solution)/shard_map/dot_general | solution.py:323
  98.6 0.0 copy-start
  98.6 0.0 copy-done.4
  98.6 1.1 multiply_convert_fusion
  99.7 0.0 copy-done
  99.7 69.1 %experts.1 = bf16[2,64,2048]{2,1,0:T(8,128)(2,1)} custom-call(bf16[2,64,2048]{2,1,0:T(8,128)(2,1)} %bitcast.86, f32[2,64,2048]{2,1,0:T(8,128)} %bitcast.80, f32[4,2,128,1]{3,2,1,0:T(8,128)} %reshape.79.share_ref, bf16[2048,1536]{1,0:T(8,128)(2,1)} %bitcast.81, bf16[768,2048]{1,0:T(8,128)(2,1)} %bitcast.85), custom_call_target="tpu_custom_call" | custom-call | tf_op jit(solution)/shard_map/experts/pallas_call | solution.py:258
  168.8 1.9 %copy.83 = bf16[128,2048]{1,0:T(8,128)(2,1)} copy(bf16[128,2048]{1,0:T(8,128)(2,1)} %bitcast.87) | data formatting | bytes 1048576
  (15 shorter events, 0.1 us)
Async XLA Ops:
  6.5 3.0 %copy-start.2 = (bf16[128,256]{1,0:T(8,128)(2,1)S(1)}, bf16[128,256]{1,0:T(8,128)(2,1)}, u32[]{:S(2)}) copy-start(bf16[128,256]{1,0:T(8,128)(2,1)} %param.16) | copy-start | bytes 196612
  6.5 3.0 %copy-start.3 = (bf16[128,256]{1,0:T(8,128)(2,1)S(1)}, bf16[128,256]{1,0:T(8,128)(2,1)}, u32[]{:S(2)}) copy-start(bf16[128,256]{1,0:T(8,128)(2,1)} %param.17) | copy-start | bytes 196612
  6.5 3.2 %copy-start.5 = (f32[128,4]{0,1:T(4,128)S(1)}, f32[128,4]{0,1:T(4,128)}, u32[]{:S(2)}) copy-start(f32[128,4]{0,1:T(4,128)} %param.25) | copy-start | bytes 6148
  6.5 3.2 %copy-start.6 = (s32[128,4]{0,1:T(4,128)S(1)}, s32[128,4]{0,1:T(4,128)}, u32[]{:S(2)}) copy-start(s32[128,4]{0,1:T(4,128)} %param.24) | copy-start | bytes 6148
  6.5 87.3 %all-gather.2.cloned.1.call-start = ((), (), s32[]{:S(2)}) async-start(), calls=%async_computation | async-start | bytes 9437184 | tf_op jit(solution)/shard_map/all_gather | solution.py:325
  37.0 56.8 %copy-start.1 = (bf16[128,2048]{1,0:T(8,128)(2,1)S(1)}, bf16[128,2048]{1,0:T(8,128)(2,1)}, u32[]{:S(2)}) copy-start(bf16[128,2048]{1,0:T(8,128)(2,1)} %param.21) | copy-start | bytes 1572868
  93.8 4.8 %copy-start.4 = (f32[2048]{0:T(1024)S(1)}, f32[2048]{0:T(1024)}, u32[]{:S(2)}) copy-start(f32[2048]{0:T(1024)} %param.23) | copy-start | bytes 24580
  98.6 1.2 copy-start
Sparse Core Ops, SparseCore 0:
  9.0 84.7 all-gather.1

commit v2 on v1

--- a/solution.py
+++ b/solution.py
@@ -12,56 +12,7 @@
 HK = 2
 HD = 128
 FF = 768
-BLK = 256
-
-
 NEGATIVE_FILL = -1e30
-
-
-def block_step(state, query_heads, keys, vals, mask):
-    top_old, sum_old, acc_old = state
-    router_logits = jnp.einsum(
-        "tgqd,kgd->tgqk", query_heads, keys, preferred_element_type=jnp.float32
-    ) * HD ** (-0.5)
-    wide_mask = mask[:, None, None, :]
-    router_logits = jnp.where(wide_mask, router_logits, NEGATIVE_FILL)
-    top_new = jnp.maximum(top_old, jnp.max(router_logits, axis=-1))
-    expert_probabilities = jnp.where(wide_mask, jnp.exp(router_logits - top_new[..., None]), 0.0)
-    shrink = jnp.exp(top_old - top_new)
-    sum_new = sum_old * shrink + jnp.sum(expert_probabilities, axis=-1)
-    acc_new = acc_old * shrink[..., None] + jnp.einsum(
-        "tgqk,kgd->tgqd",
-        expert_probabilities.astype(jnp.bfloat16),
-        vals,
-        preferred_element_type=jnp.float32,
-    )
-    return (top_new, sum_new, acc_new)
-
-
-def prefix_range(state, query_heads, cache_k, cache_v, low, high):
-    first = low // BLK
-    last = (high + BLK - 1) // BLK
-
-    def step(index, carry):
-        start = index * BLK
-        keys = lax.dynamic_slice_in_dim(cache_k, start, BLK, 0).reshape(BLK, HK, HD)
-        vals = lax.dynamic_slice_in_dim(cache_v, start, BLK, 0).reshape(BLK, HK, HD)
-        position = start + jnp.arange(BLK, dtype=jnp.int32)
-        mask = ((position >= low) & (position < high))[None, :]
-        return block_step(carry, query_heads, keys, vals, mask)
-
-    return lax.fori_loop(first, last, step, state)
-
-
-def empty_state(tok):
-    group = HQ // HK
-    return (
-        jnp.full((tok, HK, group), NEGATIVE_FILL, jnp.float32),
-        jnp.zeros((tok, HK, group), jnp.float32),
-        jnp.zeros((tok, HK, group, HD), jnp.float32),
-    )
-
-
 SPLIT = 2
 VMEM_BYTES = 58 * 1024 * 1024
 
@@ -292,6 +243,255 @@
     return out.reshape(tok, width)
 
 
+def attention_kernel(
+    nz, plen_ref, q_ref, nk_ref, nv_ref, ck_ref, cv_ref, res_ref, gain_ref, share_ref, w_hbm,
+    hidden_ref, normed_ref, shares_ref,
+    wb, keys, vals, bias, att, sh,
+    load_sem, w_send, w_recv, s_send, s_recv, ssib_send, ssib_recv,
+    q_send, q_recv, d_send, d_recv, sw_send, sw_recv,
+):
+    me, grp = lax.axis_index("dp"), lax.axis_index("grp")
+    z, c = me // 2, me % 2
+    other = 1 - c
+    r = grp % 4
+    r1 = r + 1 - 2 * (r % 2)
+    r2 = (r + 2) % 4
+    r3 = (r1 + 2) % 4
+    here, sibling, left, right = (grp, me), (grp, 2 * z + other), (grp, me - 2), (grp, me + 2)
+    peers = ((grp - r + r1, me), (grp - r + r2, me))
+    has_left, has_right = z > 0, z < nz - 1
+    tok, width = q_ref.shape
+    cached = ck_ref.shape[0]
+
+    load = pltpu.make_async_copy(w_hbm, wb.at[z, c], load_sem)
+    load.start()
+    sh[z, c] = share_ref[...]
+
+    barrier = pltpu.get_barrier_semaphore()
+
+    def greet(device):
+        pl.semaphore_signal(
+            barrier, inc=1, device_id={"grp": device[0], "dp": device[1]},
+            device_id_type=pl.DeviceIdType.MESH,
+        )
+
+    greet(sibling)
+    greet(peers[0])
+    greet(peers[1])
+    pl.when(has_left)(lambda: greet(left))
+    pl.when(has_right)(lambda: greet(right))
+    pl.semaphore_wait(barrier, 3 + jnp.where(has_left, 1, 0) + jnp.where(has_right, 1, 0))
+
+    def remote(place, send, recv, device):
+        return pltpu.make_async_remote_copy(
+            src_ref=place, dst_ref=place, send_sem=send, recv_sem=recv,
+            device_id={"grp": device[0], "dp": device[1]}, device_id_type=pl.DeviceIdType.MESH,
+        )
+
+    def w_line(b, way, device):
+        return remote(wb.at[b, c, r], w_send.at[way, b], w_recv.at[b], device)
+
+    def s_line(b, way, device):
+        return remote(sh.at[b, c], s_send.at[way, b], s_recv.at[b], device)
+
+    def s_sib(b, core):
+        return remote(sh.at[b, core], ssib_send.at[b], ssib_recv.at[b], sibling)
+
+    def w_sib(b, core, part):
+        return remote(wb.at[b, core, part], sw_send.at[b, part], sw_recv.at[b, part], sibling)
+
+    def to_peer(b, peer, part):
+        return remote(wb.at[b, c, part], q_send.at[peer, b], q_recv.at[peer, b], peers[peer])
+
+    def corner(b, half, part):
+        return remote(
+            wb.at[b, c, part, half], d_send.at[half, b], d_recv.at[half, b], peers[1 - half]
+        )
+
+    load.wait()
+    for way, ok, device in ((0, has_right, right), (1, has_left, left)):
+
+        @pl.when(ok)
+        def _(way=way, device=device):
+            w_line(z, way, device).start()
+            s_line(z, way, device).start()
+
+    s_sib(z, c).start()
+    for part in range(4):
+        w_sib(z, c, part).start()
+
+    keys[:cached] = ck_ref[...]
+    keys[cached:] = nk_ref[...]
+    vals[:cached] = cv_ref[...]
+    vals[cached:] = nv_ref[...]
+    spot = lax.broadcasted_iota(jnp.int32, bias.shape, 1)
+    row = lax.broadcasted_iota(jnp.int32, bias.shape, 0)
+    seen = (spot < plen_ref[0]) & (spot < cached) | (spot >= cached) & (spot - cached <= row)
+    bias[...] = jnp.where(seen, 0.0, NEGATIVE_FILL)
+    per_head = HQ // HK // 2
+
+    def attend(t, carry):
+        columns = pl.ds(pl.multiple_of(t * 2 * HD, 2 * HD), 2 * HD)
+        kv = pl.ds(pl.multiple_of(t // per_head * HD, HD), HD)
+        pair = q_ref[:, columns]
+        k, v = keys[:, kv], vals[:, kv]
+        for h in range(2):
+            scores = lax.dot_general(
+                pair[:, h * HD : (h + 1) * HD], k, (((1,), (1,)), ((), ())),
+                preferred_element_type=jnp.float32,
+            ) * HD ** (-0.5) + bias[...]
+            probs = jnp.exp(scores - jnp.max(scores, axis=-1, keepdims=True))
+            whole = jnp.sum(probs, axis=-1, keepdims=True)
+            out = jnp.dot(probs.astype(jnp.bfloat16), v, preferred_element_type=jnp.float32)
+            att[:, pl.ds(pl.multiple_of(t * 2 * HD + h * HD, HD), HD)] = (out / whole).astype(
+                jnp.bfloat16
+            )
+        return carry
+
+    def line_step(p):
+        b = block_at(p, z, nz)
+        w_line(b, 0, sibling).wait_recv()
+        s_line(b, 0, sibling).wait_recv()
+
+        @pl.when((b < z) & has_right)
+        def _():
+            w_line(b, 0, right).start()
+            s_line(b, 0, right).start()
+
+        @pl.when((b > z) & has_left)
+        def _():
+            w_line(b, 1, left).start()
+            s_line(b, 1, left).start()
+
+        to_peer(b, 0, r).start()
+        to_peer(b, 1, r).start()
+        w_sib(b, c, r).start()
+        s_sib(b, c).start()
+
+    def peer_step(p):
+        b = block_at(p, z, nz)
+        to_peer(b, 0, r1).wait_recv()
+        corner(b, 0, r1).start()
+        w_sib(b, c, r1).start()
+        to_peer(b, 1, r2).wait_recv()
+        corner(b, 1, r2).start()
+        w_sib(b, c, r2).start()
+
+    def corner_step(p):
+        b = block_at(p, z, nz)
+        corner(b, 0, r3).wait_recv()
+        corner(b, 1, r3).wait_recv()
+        w_sib(b, c, r3).start()
+
+    steps = HQ // 2
+    lax.fori_loop(0, steps // 2, attend, 0)
+    line_step(1)
+    lax.fori_loop(steps // 2, steps, attend, 0)
+
+    def gather(j, carry):
+        pl.when(j < nz)(lambda: line_step(j))
+        pl.when(j <= nz)(lambda: peer_step(j - 1))
+        pl.when(j > 2)(lambda: corner_step(j - 2))
+        return carry
+
+    lax.fori_loop(2, nz + 2, gather, 0)
+
+    hidden_ref[...] = res_ref[...].astype(jnp.float32)
+    depth = wb.shape[2] * wb.shape[3] * wb.shape[4]
+
+    def project(p, carry):
+        b = block_at(p, z, nz)
+        s_sib(b, other).wait_recv()
+        for part in range(4):
+            w_sib(b, other, part).wait_recv()
+        for core in range(2):
+            columns = pl.ds(pl.multiple_of((2 * b + core) * depth, 128), depth)
+            hidden_ref[...] += jnp.dot(
+                att[:, columns], wb[b, core].reshape(depth, wb.shape[5]),
+                preferred_element_type=jnp.float32,
+            )
+        return carry
+
+    lax.fori_loop(0, nz, project, 0)
+    hidden_state = hidden_ref[...]
+    scale = lax.rsqrt(jnp.mean(hidden_state * hidden_state, axis=-1, keepdims=True) + 1e-06)
+    normed_ref[...] = (hidden_state * scale * gain_ref[...]).astype(jnp.bfloat16)
+    shares_ref[...] = sh[...]
+
+    def drain(b, carry):
+        for way, ok, device in (
+            (0, (b <= z) & has_right, right), (1, (b >= z) & has_left, left),
+        ):
+
+            @pl.when(ok)
+            def _(way=way, device=device):
+                w_line(b, way, device).wait_send()
+                s_line(b, way, device).wait_send()
+
+        s_sib(b, c).wait_send()
+        for part in range(4):
+            w_sib(b, c, part).wait_send()
+
+        @pl.when(b != z)
+        def _():
+            to_peer(b, 0, r).wait_send()
+            to_peer(b, 1, r).wait_send()
+            corner(b, 0, r1).wait_send()
+            corner(b, 1, r2).wait_send()
+
+        return carry
+
+    lax.fori_loop(0, nz, drain, 0)
+
+
+def attention(
+    queries, new_keys, new_values, cache_keys, cache_values, prefix_len, residual, out_weight,
+    norm_gain, share,
+):
+    tok, width = queries.shape
+    count = share.shape[0]
+    nz = lax.axis_size("dp") // 2
+    piece = out_weight.shape[0] // 8
+    columns = out_weight.shape[1]
+    every = cache_keys.shape[0] + tok
+    vmem = pl.BlockSpec(memory_space=pltpu.VMEM)
+    half = jnp.bfloat16
+    dma = pltpu.SemaphoreType.DMA
+    return pl.pallas_call(
+        functools.partial(attention_kernel, nz),
+        out_shape=(
+            jax.ShapeDtypeStruct((tok, columns), jnp.float32),
+            jax.ShapeDtypeStruct((tok, columns), half),
+            jax.ShapeDtypeStruct((nz, 2, count, tok), jnp.float32),
+        ),
+        in_specs=[pl.BlockSpec(memory_space=pltpu.SMEM)] + [vmem] * 8
+        + [pl.BlockSpec(memory_space=pl.ANY)],
+        out_specs=(vmem, vmem, vmem),
+        scratch_shapes=[
+            pltpu.VMEM((nz, 2, 4, 2, piece, columns), half),
+            pltpu.VMEM((every, HK * HD), half),
+            pltpu.VMEM((every, HK * HD), half),
+            pltpu.VMEM((tok, every), jnp.float32),
+            pltpu.VMEM((tok, width), half),
+            pltpu.VMEM((nz, 2, count, tok), jnp.float32),
+            dma,
+            dma((2, nz)), dma((nz,)),
+            dma((2, nz)), dma((nz,)),
+            dma((nz,)), dma((nz,)),
+            dma((2, nz)), dma((2, nz)),
+            dma((2, nz)), dma((2, nz)),
+            dma((nz, 4)), dma((nz, 4)),
+        ],
+        compiler_params=pltpu.CompilerParams(
+            collective_id=2, has_side_effects=True, vmem_limit_bytes=VMEM_BYTES
+        ),
+        name="attention",
+    )(
+        prefix_len, queries, new_keys, new_values, cache_keys, cache_values, residual,
+        norm_gain.reshape(1, columns), share, out_weight.reshape(4, 2, piece, columns),
+    )
+
+
 def local(
     queries,
     new_keys,
@@ -307,34 +507,15 @@
     expert_gate_up,
     expert_down,
 ):
-    tok = queries.shape[0]
-    group = HQ // HK
-    query_heads = queries.reshape(tok, HK, group, HD)
-    plen = prefix_len[0]
-    state = prefix_range(
-        empty_state(tok), query_heads, cache_keys, cache_values, jnp.int32(0), plen
-    )
-    row = jnp.arange(tok, dtype=jnp.int32)
-    causal = row[None, :] <= row[:, None]
-    state = block_step(
-        state, query_heads, new_keys.reshape(tok, HK, HD), new_values.reshape(tok, HK, HD), causal
-    )
-    attended = (state[2] / state[1][..., None]).reshape(tok, HQ * HD).astype(jnp.bfloat16)
-    projected = jnp.dot(
-        attended,
-        lax.all_gather(out_weight, "dp", axis=0, tiled=True),
-        preferred_element_type=jnp.float32,
-    )
-    hidden_state = residual.astype(jnp.float32) + projected
-    scale = lax.rsqrt(jnp.mean(hidden_state * hidden_state, axis=-1, keepdims=True) + 1e-06)
-    normed = (hidden_state * scale * norm_gain).astype(jnp.bfloat16)
     count = expert_gate_up.shape[0] * lax.axis_size("dp")
     route_weights = gate_scores / jnp.sum(gate_scores, axis=-1, keepdims=True)
     chosen = expert_ids[:, :, None] == jnp.arange(count, dtype=jnp.int32)
-    share = jnp.sum(jnp.where(chosen, route_weights[:, :, None], 0.0), axis=1)
-    shares = lax.all_gather(share, "dp", axis=0, tiled=True)
-    mine = jnp.arange(count, dtype=jnp.int32) == lax.axis_index("dp")
-    share = jnp.sum(jnp.where(mine, shares, 0.0), axis=1)
+    share = jnp.sum(jnp.where(chosen, route_weights[:, :, None], 0.0), axis=1).T
+    hidden_state, normed, shares = attention(
+        queries, new_keys, new_values, cache_keys, cache_values, prefix_len, residual, out_weight,
+        norm_gain, share,
+    )
+    share = lax.dynamic_index_in_dim(shares, lax.axis_index("dp"), 2, keepdims=False)
     return experts(normed, hidden_state, share, expert_gate_up[0], expert_down[0])
 
 

time: 178 us -> 125 us (0.70)
  waiting for transfers between devices: 55.5 us -> 0 us
  Pallas kernels: 69.1 us -> 117 us
  blocking collectives: 15.8 us -> 0 us
  between operations: 14.2 us -> 0.67 us
  matrix products: 11.6 us -> 0 us
  local copies, waits for them, and re-layouts: 7.36 us -> 4.05 us
    all_gather x1 -> x0, waiting for transfers between devices: 54.8 us -> none  [local(): lax.all_gather(out_weight, 'dp', axis=0, tiled=True)]
    pallas_call x0 -> x1, Pallas kernels: none -> 48.1 us  [attention(): pl.pallas_call(functools.partial(attention_kernel, nz), out_shape=(jax.Sh...]
    all_gather x1 -> x0, blocking collectives: 15.8 us -> none  [local(): shares = lax.all_gather(share, 'dp', axis=0, tiled=True)]
    dot_general x5 -> x0, matrix products: 11.6 us -> none  [the longest x2 4.89 us: block_step(): jnp.einsum('tgqk,kgd->tgqd', expert_probabilities.astype(jnp.bfloat16), v...]
  transfers between devices with their start and end apart: 1 -> 0, of which waited for: 1 -> 0; matrix products, arithmetic and copies ran while one was open for 9% -> 0% of each run, Pallas kernels for 0% -> 0%
where the time goes in v2:
time: 125 us; the launch traced here: 124 us
  Pallas kernels  117 us (94%)
  local copies, waits for them, and re-layouts  4.05 us (3%)
  other arithmetic  2.67 us (2%)
    pallas_call x1, Pallas kernels, experts(): pl.pallas_call(functools.partial(experts_kernel, nz, split), out_shape=ja...  68.8 us
    pallas_call x1, Pallas kernels, attention(): pl.pallas_call(functools.partial(attention_kernel, nz), out_shape=(jax.Sh...  48.1 us

profile of v2, /device:TPU:0, one launch (start us, length us, event | category | flops | bytes accessed | tf_op | source)
XLA Modules:
  0.0 124.3 jit_solution(2587110304444282328)
XLA Ops:
  0.7 0.7 reduce_sum.18
  1.4 0.7 broadcast_divide_fusion
  2.0 1.3 %select_reduce_fusion = f32[128,8]{0,1:T(8,128)} fusion(f32[128,4]{0,1:T(4,128)S(1)} %broadcast_divide_fusion, s32[128,4]{0,1:T(4,128)} %param.22), kind=kLoop, calls=%fused_computation | loop fusion | flops 11264 | bytes 8192 | tf_op jit(solution)/shard_map/reduce_sum | solution.py:513
  3.3 48.1 %attention.1 = (f32[128,2048]{1,0:T(8,128)}, bf16[128,2048]{1,0:T(8,128)(2,1)}, f32[4,2,8,128]{3,2,1,0:T(8,128)}) custom-call(s32[1]{0:T(128)S(6)} %copy.23.plen_ref, bf16[128,2048]{1,0:T(8,128)(2,1)} %q_ref.1, bf16[128,256]{1,0:T(8,128)(2,1)} %nk_ref.1, bf16[128,256]{1,0:T(8,128)(2,1)} %nv_ref.1, bf16[1024,256]{1,0:T(8,128)(2,1)} %ck_ref.1, ...), custom_call_target="tpu_custom_call" | custom-call | tf_op jit(solution)/shard_map/attention/pallas_call | solution.py:460
  51.4 0.8 dynamic-slice_reduce_fusion
  52.2 0.1 reshape.29
  52.3 1.3 %reshape.32.share_ref = f32[4,2,128,1]{3,2,1,0:T(8,128)} reshape(f32[4,2,2,64]{3,2,1,0:T(2,128)S(1)} %copy.20) | data formatting | bytes 8192 | tf_op jit(solution)/shard_map/reshape | solution.py:204
  53.6 68.8 %experts.1 = bf16[2,64,2048]{2,1,0:T(8,128)(2,1)} custom-call(bf16[2,64,2048]{2,1,0:T(8,128)(2,1)} %bitcast.14, f32[2,64,2048]{2,1,0:T(8,128)} %bitcast.12, f32[4,2,128,1]{3,2,1,0:T(8,128)} %reshape.32.share_ref, bf16[2048,1536]{1,0:T(8,128)(2,1)} %bitcast.9, bf16[768,2048]{1,0:T(8,128)(2,1)} %bitcast.10), custom_call_target="tpu_custom_call" | custom-call | tf_op jit(solution)/shard_map/experts/pallas_call | solution.py:209
  122.4 1.9 %copy.24 = bf16[128,2048]{1,0:T(8,128)(2,1)} copy(bf16[128,2048]{1,0:T(8,128)(2,1)} %bitcast.11) | data formatting | bytes 1048576
  (1 shorter events, 0.0 us)

commit v3 on v2

--- a/solution.py
+++ b/solution.py
@@ -83,16 +83,6 @@
             total.at[b, s], line_sum.at[way, b, s], line_send.at[b, s], line_recv.at[way, b, s], device
         )
 
-    def send_own(s, carry):
-        pl.when(has_right)(lambda: x_line(z, s, 0, right).start())
-        pl.when(has_left)(lambda: x_line(z, s, 1, left).start())
-        x_sib(z, s, c).start()
-        return carry
-
-    lax.fori_loop(0, split, send_own, 0)
-    load_gu.wait()
-    load_down.wait()
-
     def send_sum(b, s):
         pl.when(b > z)(lambda: sum_line(b, s, 0, right).start())
         pl.when(b < z)(lambda: sum_line(b, s, 1, left).start())
@@ -100,16 +90,38 @@
     def is_end(b):
         return ((b > z) & (z == 0)) | ((b < z) & (z == nz - 1))
 
+    mirror = nz - 1 - z
+
+    def send_half(s, ok_right, ok_left):
+        pl.when(has_right & ok_right)(lambda: x_line(z, s, 0, right).start())
+        pl.when(has_left & ok_left)(lambda: x_line(z, s, 1, left).start())
+
+    send_half(0, True, True)
+    x_sib(z, 0, c).start()
+    x_sib(z, 1, c).start()
+
     def compute(i, carry):
-        p, s = i // split, i % split
-        b = block_at(p, z, nz)
-
-        @pl.when(p > 0)
+        slot, side, s = i // 4, i % 2, i // 2 % 2
+        pl.when(i % 4 == 0)(lambda: send_half(1, slot == 2 * z + 1, slot == 2 * mirror + 1))
+        reach = jnp.where(side == 0, z, mirror)
+        near = jnp.where(s == 0, reach - slot, slot - 1 - reach)
+        b = jnp.where(slot == 0, z, jnp.where(side == 0, near, nz - 1 - near))
+        due = jnp.where(slot == 0, side == 0, (near >= 0) & (near < reach))
+        pl.when(due)(lambda: compute_block(slot, b, s))
+        return carry
+
+    def compute_block(slot, b, s):
+        @pl.when(slot > 0)
         def _():
             x_line(b, s, 0, sibling).wait_recv()
             pl.when((b < z) & has_right)(lambda: x_line(b, s, 0, right).start())
             pl.when((b > z) & has_left)(lambda: x_line(b, s, 1, left).start())
             x_sib(b, s, c).start()
+
+        @pl.when((slot == 0) & (s == 0))
+        def _():
+            load_gu.wait()
+            load_down.wait()
 
         x_sib(b, s, other).wait_recv()
         x = xs[b, s].reshape(2 * rows, width)
@@ -137,9 +149,7 @@
             ).astype(jnp.bfloat16)
             send_sum(b, s)
 
-        return carry
-
-    lax.fori_loop(0, nz * split, compute, 0)
+    lax.fori_loop(0, 4 * (2 * nz - 1), compute, 0)
 
     def add_and_pass(b, s, way):
         y_sib(b, s).wait_recv()
@@ -152,15 +162,15 @@
         send_sum(b, s)
 
     def pass_on(i, carry):
-        hop, s = i // split, i % split
-        from_left, from_right = hop - z, 2 * (nz - 1) - z - hop
-        pl.when(has_left & (from_left > z) & (from_left < nz))(lambda: add_and_pass(from_left, s, 0))
-        pl.when(has_right & (from_right < z) & (from_right >= 0))(
-            lambda: add_and_pass(from_right, s, 1)
-        )
-        return carry
-
-    lax.fori_loop(split, (2 * nz - 1) * split, pass_on, 0)
+        slot, side, s = i // 4, i % 2, i // 2 % 2
+        reach = jnp.where(side == 0, z, mirror)
+        far = jnp.where(s == 0, slot - reach, 2 * nz - 1 + reach - slot)
+        b = jnp.where(side == 0, far, nz - 1 - far)
+        due = (reach > 0) & (far > reach) & (far < nz)
+        pl.when(due)(lambda: add_and_pass(b, s, side))
+        return carry
+
+    lax.fori_loop(4, 4 * 3 * nz, pass_on, 0)
 
     def finish(s, carry):
         y_sib(z, s).wait_recv()

time: 125 us -> 123 us (0.984)
  Pallas kernels: 117 us -> 115 us
    pallas_call x1, Pallas kernels: 68.8 us -> 66.8 us  [experts(): pl.pallas_call(functools.partial(experts_kernel, nz, split), out_shape=ja...]
where the time goes in v3:
time: 123 us; the launch traced here: 122 us
  Pallas kernels  115 us (93%)
  local copies, waits for them, and re-layouts  4.05 us (3%)
  other arithmetic  2.67 us (2%)
    pallas_call x1, Pallas kernels, experts(): pl.pallas_call(functools.partial(experts_kernel, nz, split), out_shape=ja...  66.8 us
    pallas_call x1, Pallas kernels, attention(): pl.pallas_call(functools.partial(attention_kernel, nz), out_shape=(jax.Sh...  48.1 us

profile of v3, /device:TPU:0, one launch (start us, length us, event | category | flops | bytes accessed | tf_op | source)
XLA Modules:
  0.0 122.3 jit_solution(10856972146649693428)
XLA Ops:
  0.7 0.7 reduce_sum.18
  1.4 0.7 broadcast_divide_fusion
  2.0 1.3 %select_reduce_fusion = f32[128,8]{0,1:T(8,128)} fusion(f32[128,4]{0,1:T(4,128)S(1)} %broadcast_divide_fusion, s32[128,4]{0,1:T(4,128)} %param.22), kind=kLoop, calls=%fused_computation | loop fusion | flops 11264 | bytes 8192 | tf_op jit(solution)/shard_map/reduce_sum | solution.py:523
  3.3 48.1 %attention.1 = (f32[128,2048]{1,0:T(8,128)}, bf16[128,2048]{1,0:T(8,128)(2,1)}, f32[4,2,8,128]{3,2,1,0:T(8,128)}) custom-call(s32[1]{0:T(128)S(6)} %copy.23.plen_ref, bf16[128,2048]{1,0:T(8,128)(2,1)} %q_ref.1, bf16[128,256]{1,0:T(8,128)(2,1)} %nk_ref.1, bf16[128,256]{1,0:T(8,128)(2,1)} %nv_ref.1, bf16[1024,256]{1,0:T(8,128)(2,1)} %ck_ref.1, ...), custom_call_target="tpu_custom_call" | custom-call | tf_op jit(solution)/shard_map/attention/pallas_call | solution.py:470
  51.4 0.8 dynamic-slice_reduce_fusion
  52.2 0.1 reshape.29
  52.3 1.3 %reshape.32.share_ref = f32[4,2,128,1]{3,2,1,0:T(8,128)} reshape(f32[4,2,2,64]{3,2,1,0:T(2,128)S(1)} %copy.20) | data formatting | bytes 8192 | tf_op jit(solution)/shard_map/reshape | solution.py:214
  53.6 66.8 %experts.1 = bf16[2,64,2048]{2,1,0:T(8,128)(2,1)} custom-call(bf16[2,64,2048]{2,1,0:T(8,128)(2,1)} %bitcast.14, f32[2,64,2048]{2,1,0:T(8,128)} %bitcast.12, f32[4,2,128,1]{3,2,1,0:T(8,128)} %reshape.32.share_ref, bf16[2048,1536]{1,0:T(8,128)(2,1)} %bitcast.9, bf16[768,2048]{1,0:T(8,128)(2,1)} %bitcast.10), custom_call_target="tpu_custom_call" | custom-call | tf_op jit(solution)/shard_map/experts/pallas_call | solution.py:219
  120.4 1.9 %copy.24 = bf16[128,2048]{1,0:T(8,128)(2,1)} copy(bf16[128,2048]{1,0:T(8,128)(2,1)} %bitcast.11) | data formatting | bytes 1048576
  (1 shorter events, 0.0 us)

commit v4 on v3

--- a/solution.py
+++ b/solution.py
@@ -398,18 +398,10 @@
     line_step(1)
     lax.fori_loop(steps // 2, steps, attend, 0)
 
-    def gather(j, carry):
-        pl.when(j < nz)(lambda: line_step(j))
-        pl.when(j <= nz)(lambda: peer_step(j - 1))
-        pl.when(j > 2)(lambda: corner_step(j - 2))
-        return carry
-
-    lax.fori_loop(2, nz + 2, gather, 0)
-
     hidden_ref[...] = res_ref[...].astype(jnp.float32)
     depth = wb.shape[2] * wb.shape[3] * wb.shape[4]
 
-    def project(p, carry):
+    def project(p):
         b = block_at(p, z, nz)
         s_sib(b, other).wait_recv()
         for part in range(4):
@@ -420,9 +412,16 @@
                 att[:, columns], wb[b, core].reshape(depth, wb.shape[5]),
                 preferred_element_type=jnp.float32,
             )
-        return carry
-
-    lax.fori_loop(0, nz, project, 0)
+
+    def gather(j, carry):
+        pl.when(j < nz)(lambda: line_step(j))
+        pl.when(j <= nz)(lambda: peer_step(j - 1))
+        pl.when(j > 2)(lambda: corner_step(j - 2))
+        pl.when(j > 2)(lambda: project(j - 3))
+        return carry
+
+    lax.fori_loop(2, nz + 2, gather, 0)
+    project(nz - 1)
     hidden_state = hidden_ref[...]
     scale = lax.rsqrt(jnp.mean(hidden_state * hidden_state, axis=-1, keepdims=True) + 1e-06)
     normed_ref[...] = (hidden_state * scale * gain_ref[...]).astype(jnp.bfloat16)

time: 123 us -> 124 us (level)
    pallas_call x1, Pallas kernels: 66.8 us -> 69 us  [experts(): pl.pallas_call(functools.partial(experts_kernel, nz, split), out_shape=ja...]
where the time goes in v4:
time: 124 us
  Pallas kernels  116 us (94%)
  local copies, waits for them, and re-layouts  4.05 us (3%)
  other arithmetic  2.67 us (2%)
    pallas_call x1, Pallas kernels, experts(): pl.pallas_call(functools.partial(experts_kernel, nz, split), out_shape=ja...  69 us
    pallas_call x1, Pallas kernels, attention(): pl.pallas_call(functools.partial(attention_kernel, nz), out_shape=(jax.Sh...  47.1 us

profile of v4, /device:TPU:0, one launch (start us, length us, event | category | flops | bytes accessed | tf_op | source)
XLA Modules:
  0.0 123.5 jit_solution(8185885400739542956)
XLA Ops:
  0.7 0.7 reduce_sum.18
  1.4 0.7 broadcast_divide_fusion
  2.0 1.3 %select_reduce_fusion = f32[128,8]{0,1:T(8,128)} fusion(f32[128,4]{0,1:T(4,128)S(1)} %broadcast_divide_fusion, s32[128,4]{0,1:T(4,128)} %param.22), kind=kLoop, calls=%fused_computation | loop fusion | flops 11264 | bytes 8192 | tf_op jit(solution)/shard_map/reduce_sum | solution.py:522
  3.3 47.1 %attention.1 = (f32[128,2048]{1,0:T(8,128)}, bf16[128,2048]{1,0:T(8,128)(2,1)}, f32[4,2,8,128]{3,2,1,0:T(8,128)}) custom-call(s32[1]{0:T(128)S(6)} %copy.23.plen_ref, bf16[128,2048]{1,0:T(8,128)(2,1)} %q_ref.1, bf16[128,256]{1,0:T(8,128)(2,1)} %nk_ref.1, bf16[128,256]{1,0:T(8,128)(2,1)} %nv_ref.1, bf16[1024,256]{1,0:T(8,128)(2,1)} %ck_ref.1, ...), custom_call_target="tpu_custom_call" | custom-call | tf_op jit(solution)/shard_map/attention/pallas_call | solution.py:469
  50.5 0.8 dynamic-slice_reduce_fusion
  51.3 0.1 reshape.29
  51.4 1.3 %reshape.32.share_ref = f32[4,2,128,1]{3,2,1,0:T(8,128)} reshape(f32[4,2,2,64]{3,2,1,0:T(2,128)S(1)} %copy.20) | data formatting | bytes 8192 | tf_op jit(solution)/shard_map/reshape | solution.py:214
  52.6 69.0 %experts.1 = bf16[2,64,2048]{2,1,0:T(8,128)(2,1)} custom-call(bf16[2,64,2048]{2,1,0:T(8,128)(2,1)} %bitcast.14, f32[2,64,2048]{2,1,0:T(8,128)} %bitcast.12, f32[4,2,128,1]{3,2,1,0:T(8,128)} %reshape.32.share_ref, bf16[2048,1536]{1,0:T(8,128)(2,1)} %bitcast.9, bf16[768,2048]{1,0:T(8,128)(2,1)} %bitcast.10), custom_call_target="tpu_custom_call" | custom-call | tf_op jit(solution)/shard_map/experts/pallas_call | solution.py:219
  121.6 1.9 %copy.24 = bf16[128,2048]{1,0:T(8,128)(2,1)} copy(bf16[128,2048]{1,0:T(8,128)(2,1)} %bitcast.11) | data formatting | bytes 1048576
  (1 shorter events, 0.0 us)
